TPU v7x, 128 devices: a whole 4x4x4 slice. The times are simulated.
128 devices in a mesh: row: 16 (over x_hi, z, core), col: 8 (over y, x_lo).
Axes of the slice: x: 4 (x_hi: 2, x_lo: 2; x = x_hi * 2 + x_lo), y: 4, z: 4, core: 2. Of those that a mesh axis runs over, the one named last changes fastest.
Arguments:
- vector: float32 [2048, 16384], P('row', 'col')
- previous: float32 [2048, 16384], P('row', 'col'), may hold values from -6 to 6
- beta_prev: float32 [1], replicated, may hold values from 0.5 to 1.5
- hubbard_u: float32 [1], replicated, may hold values from 1 to 4
- up_patterns: float32 [16, 128, 128], replicated
- down_patterns: float32 [16, 128, 128], replicated
- up_cols: int32 [16, 12], replicated, may hold values from 0 to 15
- up_pats: int32 [16, 12], replicated, may hold values from 0 to 15
- down_cols: int32 [128, 12], replicated, may hold values from 0 to 127
- down_pats: int32 [128, 12], replicated, may hold values from 0 to 15
- up_occupied: int32 [20, 2048], P(None, 'row'), may hold values 0 or 1
- down_occupied: int32 [20, 16384], P(None, 'col'), may hold values 0 or 1
Outputs:
- next_vector: float32 [2048, 16384], P('row', 'col')
- coefficients: float32 [2], replicated
All inputs are finite; a program needn't handle non-finite values. No bound on the sum of `up_occupied` or of `down_occupied` on one device may be relied on, other than what follows from the above.
Results may differ from a plain program's by a relative error of at most 0.0004.
Values sent between devices are 32-bit elements; how exact they have to be, the bound alone decides.
A program may use at most 320 MiB of HBM per device.

v0:
```python
import jax
import jax.numpy as jnp
from jax import lax
from jax.sharding import PartitionSpec as P


def local(
    vector,
    previous,
    beta_prev,
    hubbard_u,
    up_patterns,
    down_patterns,
    up_cols,
    up_pats,
    down_cols,
    down_pats,
    up_occupied,
    down_occupied,
):
    hi = lax.Precision.HIGHEST
    block = up_patterns.shape[1]
    hops = up_cols.shape[1]
    local_rows, local_cols = vector.shape
    columns = lax.all_to_all(vector, "row", split_axis=1, concat_axis=0, tiled=True)
    width = columns.shape[1]
    up_blocks = up_cols.shape[0]
    upper = columns.reshape(up_blocks, block, width)
    up_acc = jnp.zeros((up_blocks, block, width), jnp.float32)
    for h in range(hops):
        up_acc = up_acc + jnp.einsum(
            "ipq,iqd->ipd", up_patterns[up_pats[:, h]], upper[up_cols[:, h]], precision=hi
        )
    up_term = lax.all_to_all(
        up_acc.reshape(up_blocks * block, width), "row", split_axis=0, concat_axis=1, tiled=True
    )
    down_blocks = down_cols.shape[0]
    slab = lax.all_to_all(vector, "col", split_axis=0, concat_axis=1, tiled=True)
    thin_rows = slab.shape[0]
    lower = slab.reshape(thin_rows, down_blocks, block)
    down_acc = jnp.zeros((thin_rows, down_blocks, block), jnp.float32)
    for h in range(hops):
        down_acc = down_acc + jnp.einsum(
            "ujq,jpq->ujp", lower[:, down_cols[:, h]], down_patterns[down_pats[:, h]], precision=hi
        )
    down_term = lax.all_to_all(
        down_acc.reshape(thin_rows, down_blocks * block),
        "col",
        split_axis=1,
        concat_axis=0,
        tiled=True,
    )
    doubles = jnp.dot(
        up_occupied.astype(jnp.float32).T, down_occupied.astype(jnp.float32), precision=hi
    )
    image = up_term + down_term + hubbard_u[0] * doubles * vector
    total = local_rows * lax.axis_size("row") * (local_cols * lax.axis_size("col"))
    weight_prev = beta_prev[0]
    cross, square = lax.psum((jnp.sum(vector * image), jnp.sum(vector * vector)), ("row", "col"))
    alpha = cross / square
    residual = image - alpha * vector - weight_prev * previous
    energy = lax.psum(jnp.sum(residual * residual), ("row", "col"))
    scale = jnp.sqrt(energy / total + 1e-06)
    return (residual / scale, jnp.stack([alpha, scale]))


def solution(mesh):
    in_specs = (
        P("row", "col"),
        P("row", "col"),
        P(),
        P(),
        P(),
        P(),
        P(),
        P(),
        P(),
        P(),
        P(None, "row"),
        P(None, "col"),
    )
    out_specs = (P("row", "col"), P())
    return jax.shard_map(local, mesh=mesh, in_specs=in_specs, out_specs=out_specs, check_vma=False)
```

profile of v0, /device:TPU:1, one launch (start us, length us, event | category | flops | bytes accessed | tf_op | source)
XLA Modules:
  0.0 503.4 jit_solution(7962012478442173139)
XLA Ops:
  0.6 6.1 %all-to-all-start.2 = ((f32[8,16,2048]{2,1,0:T(8,128)}), f32[8,16,2048]{2,1,0:T(8,128)}, u32[]{:S(2)}, u32[]{:S(2)}) async-start(f32[8,16,2048]{2,1,0:T(8,128)} %bitcast.164), calls=%async_computation.2 | async-start | bytes 2097152 | tf_op jit(solution)/shard_map/all_to_all | solution.py:38
  12.1 4.4 gather_fusion.24
  16.5 4.3 gather_fusion.26
  20.8 4.3 gather_fusion.28
  25.1 4.4 gather_fusion.30
  29.5 4.3 gather_fusion.32
  33.8 4.3 gather_fusion.34
  38.1 4.3 gather_fusion.36
  42.4 4.3 gather_fusion.38
  46.7 4.3 gather_fusion.40
  51.0 4.3 gather_fusion.42
  55.4 4.3 gather_fusion.44
  59.7 4.3 gather_fusion.46
  84.0 9.1 %all-to-all-start = ((f32[128,16,128]{2,0,1:T(8,128)}), f32[128,16,128]{2,0,1:T(8,128)S(1)}, u32[]{:S(2)}, u32[]{:S(2)}) async-start(f32[128,16,128]{2,0,1:T(8,128)} %copy.51), calls=%async_computation | async-start | bytes 2097152 | tf_op jit(solution)/shard_map/all_to_all | solution.py:25
  118.8 15.6 %fusion.14 = f32[128,128,16]{1,2,0:T(8,128)S(1)} fusion(f32[128,128,128]{2,1,0:T(8,128)} %gather_fusion.24, f32[128,16,128]{2,1,0:T(8,128)} %gather_fusion.25), kind=kOutput, calls=%fused_computation.86 | convolution fusion | flops 402653184 | bytes 10485760 | tf_op jit(solution)/shard_map/ujq,jpq->ujp/dot_general | solution.py:43
  134.4 15.7 %convolution_add_fusion.21 = f32[128,128,16]{1,2,0:T(8,128)S(1)} fusion(f32[128,128,16]{1,2,0:T(8,128)S(1)} %fusion.14, f32[128,128,128]{2,1,0:T(8,128)} %gather_fusion.26, f32[128,16,128]{2,1,0:T(8,128)S(1)} %copy-done.33), kind=kOutput, calls=%fused_computation.73 | convolution fusion | flops 402915328 | bytes 11534336 | tf_op jit(solution)/shard_map/ujq,jpq->ujp/dot_general | solution.py:43
  150.2 15.7 %convolution_add_fusion.20 = f32[128,128,16]{1,2,0:T(8,128)S(1)} fusion(f32[128,128,16]{1,2,0:T(8,128)S(1)} %convolution_add_fusion.21, f32[128,128,128]{2,1,0:T(8,128)} %gather_fusion.28, f32[128,16,128]{2,1,0:T(8,128)S(1)} %copy-done.32), kind=kOutput, calls=%fused_computation.72 | convolution fusion | flops 402915328 | bytes 11534336 | tf_op jit(solution)/shard_map/ujq,jpq->ujp/dot_general | solution.py:43
  166.0 13.1 %convolution_add_fusion.19 = f32[128,128,16]{1,2,0:T(8,128)S(1)} fusion(f32[128,128,16]{1,2,0:T(8,128)S(1)} %convolution_add_fusion.20, f32[128,128,128]{2,1,0:T(8,128)S(1)} %bitcast.163, f32[128,16,128]{2,1,0:T(8,128)S(1)} %copy-done.31), kind=kOutput, calls=%fused_computation.71 | convolution fusion | flops 402915328 | bytes 11534336 | tf_op jit(solution)/shard_map/ujq,jpq->ujp/dot_general | solution.py:43
  179.1 14.4 %convolution_add_fusion.18 = f32[128,128,16]{1,2,0:T(8,128)} fusion(f32[128,128,16]{1,2,0:T(8,128)S(1)} %convolution_add_fusion.19, f32[128,128,128]{2,1,0:T(8,128)S(1)} %bitcast.161, f32[128,16,128]{2,1,0:T(8,128)S(1)} %copy-done.30), kind=kOutput, calls=%fused_computation.70 | convolution fusion | flops 402915328 | bytes 11534336 | tf_op jit(solution)/shard_map/ujq,jpq->ujp/dot_general | solution.py:43
  193.6 14.6 %convolution_add_fusion.17 = f32[128,128,16]{1,2,0:T(8,128)S(1)} fusion(f32[128,128,16]{1,2,0:T(8,128)} %convolution_add_fusion.18, f32[128,128,128]{2,1,0:T(8,128)S(1)} %bitcast.159, f32[128,16,128]{2,1,0:T(8,128)S(1)} %copy-done.29), kind=kOutput, calls=%fused_computation.69 | convolution fusion | flops 402915328 | bytes 11534336 | tf_op jit(solution)/shard_map/ujq,jpq->ujp/dot_general | solution.py:43
  208.2 13.1 %convolution_add_fusion.16 = f32[128,128,16]{1,2,0:T(8,128)S(1)} fusion(f32[128,128,16]{1,2,0:T(8,128)S(1)} %convolution_add_fusion.17, f32[128,128,128]{2,1,0:T(8,128)S(1)} %bitcast.157, f32[128,16,128]{2,1,0:T(8,128)S(1)} %copy-done.28), kind=kOutput, calls=%fused_computation.68 | convolution fusion | flops 402915328 | bytes 11534336 | tf_op jit(solution)/shard_map/ujq,jpq->ujp/dot_general | solution.py:43
  221.3 13.2 %convolution_add_fusion.15 = f32[128,128,16]{1,2,0:T(8,128)S(1)} fusion(f32[128,128,16]{1,2,0:T(8,128)S(1)} %convolution_add_fusion.16, f32[128,128,128]{2,1,0:T(8,128)S(1)} %bitcast.155, f32[128,16,128]{2,1,0:T(8,128)S(1)} %copy-done.27), kind=kOutput, calls=%fused_computation.67 | convolution fusion | flops 402915328 | bytes 11534336 | tf_op jit(solution)/shard_map/ujq,jpq->ujp/dot_general | solution.py:43
  234.6 13.4 %convolution_add_fusion.14 = f32[128,128,16]{1,2,0:T(8,128)S(1)} fusion(f32[128,128,16]{1,2,0:T(8,128)S(1)} %convolution_add_fusion.15, f32[128,128,128]{2,1,0:T(8,128)S(1)} %bitcast.153, f32[128,16,128]{2,1,0:T(8,128)S(1)} %copy-done.26), kind=kOutput, calls=%fused_computation.66 | convolution fusion | flops 402915328 | bytes 11534336 | tf_op jit(solution)/shard_map/ujq,jpq->ujp/dot_general | solution.py:43
  248.1 14.1 %convolution_add_fusion.13 = f32[128,128,16]{1,2,0:T(8,128)} fusion(f32[128,128,16]{1,2,0:T(8,128)S(1)} %convolution_add_fusion.14, f32[128,128,128]{2,1,0:T(8,128)S(1)} %bitcast.151, f32[128,16,128]{2,1,0:T(8,128)S(1)} %copy-done.25), kind=kOutput, calls=%fused_computation.65 | convolution fusion | flops 402915328 | bytes 11534336 | tf_op jit(solution)/shard_map/ujq,jpq->ujp/dot_general | solution.py:43
  281.9 2.9 convolution_add_fusion.10
  299.9 7.2 %all-to-all-start.1 = ((f32[16,128,128]{2,1,0:T(8,128)}), f32[16,128,128]{2,1,0:T(8,128)S(1)}, u32[]{:S(2)}, u32[]{:S(2)}) async-start(f32[16,128,128]{2,1,0:T(8,128)} %convolution_add_fusion), calls=%async_computation.1 | async-start | bytes 2097152 | tf_op jit(solution)/shard_map/all_to_all | solution.py:34
  307.1 15.5 %convolution_add_fusion.12 = f32[128,128,16]{1,2,0:T(8,128)S(1)} fusion(f32[128,128,16]{1,2,0:T(8,128)} %convolution_add_fusion.13, f32[128,128,128]{2,1,0:T(8,128)} %gather_fusion.44, f32[128,16,128]{2,1,0:T(8,128)S(1)} %copy-done.24), kind=kOutput, calls=%fused_computation.64 | convolution fusion | flops 402915328 | bytes 11534336 | tf_op jit(solution)/shard_map/ujq,jpq->ujp/dot_general | solution.py:43
  322.6 15.4 %fusion.2 = f32[16,128,128]{2,0,1:T(8,128)S(1)} fusion(f32[128,128,16]{1,2,0:T(8,128)S(1)} %convolution_add_fusion.12, f32[128,128,128]{2,1,0:T(8,128)} %gather_fusion.46, f32[128,16,128]{2,1,0:T(8,128)S(1)} %copy-done.23), kind=kOutput, calls=%fused_computation.63 | convolution fusion | flops 402915328 | bytes 11534336 | tf_op jit(solution)/shard_map/ujq,jpq->ujp/dot_general | solution.py:43
  343.3 5.1 %all-to-all-start.3 = ((f32[16,8,2048]{2,0,1:T(8,128)}), f32[16,8,2048]{2,0,1:T(8,128)S(1)}, u32[]{:S(2)}, u32[]{:S(2)}) async-start(f32[16,8,2048]{2,0,1:T(8,128)} %copy.67), calls=%async_computation.3 | async-start | bytes 2097152 | tf_op jit(solution)/shard_map/all_to_all | solution.py:46
  355.0 9.0 %all-to-all-done.3 = f32[16,8,2048]{2,0,1:T(8,128)S(1)} async-done(((f32[16,8,2048]{2,0,1:T(8,128)}), f32[16,8,2048]{2,0,1:T(8,128)S(1)}, u32[]{:S(2)}, u32[]{:S(2)}) %all-to-all-start.3) | async-done | bytes 1048608 | tf_op jit(solution)/shard_map/all_to_all | solution.py:46
  368.2 65.9 %all-reduce = (f32[]{:T(128)}, f32[]{:T(128)}) all-reduce(f32[]{:T(128)} %get-tuple-element.3, f32[]{:T(128)} %get-tuple-element.2), channel_id=1, replica_groups=mesh['row'=16,'col'=8] {'row','col'}, use_global_device_ids=true, to_apply=%region_1.0 | all-reduce | flops 2 | bytes 16 | tf_op jit(solution)/shard_map/psum | solution.py:59
  437.9 62.7 %psum.23 = f32[]{:T(128)} all-reduce(f32[]{:T(128)} %get-tuple-element.30), channel_id=1, replica_groups=mesh['row'=16,'col'=8] {'row','col'}, use_global_device_ids=true, to_apply=%region_5.0 | all-reduce | flops 1 | bytes 8 | tf_op jit(solution)/shard_map/psum | solution.py:62
  (202 shorter events, 104.3 us)
Async XLA Ops:
  0.6 83.4 %all-to-all-start.2 = ((f32[8,16,2048]{2,1,0:T(8,128)}), f32[8,16,2048]{2,1,0:T(8,128)}, u32[]{:S(2)}, u32[]{:S(2)}) async-start(f32[8,16,2048]{2,1,0:T(8,128)} %bitcast.164), calls=%async_computation.2 | async-start | bytes 2097152 | tf_op jit(solution)/shard_map/all_to_all | solution.py:38
  84.0 178.2 %all-to-all-start = ((f32[128,16,128]{2,0,1:T(8,128)}), f32[128,16,128]{2,0,1:T(8,128)S(1)}, u32[]{:S(2)}, u32[]{:S(2)}) async-start(f32[128,16,128]{2,0,1:T(8,128)} %copy.51), calls=%async_computation | async-start | bytes 2097152 | tf_op jit(solution)/shard_map/all_to_all | solution.py:25
  118.8 15.6 %copy-start.33 = (f32[128,16,128]{2,1,0:T(8,128)S(1)}, f32[128,16,128]{2,1,0:T(8,128)}, u32[]{:S(2)}) copy-start(f32[128,16,128]{2,1,0:T(8,128)} %gather_fusion.27) | copy-start | bytes 3145732
  118.8 47.1 %slice-start.12 = ((s8[8388608]{0:T(1024)(128)(4,1)}), s8[4194304]{0:T(1024)(128)(4,1)S(1)}, s32[]{:S(2)}) async-start(s8[8388608]{0:T(1024)(128)(4,1)} %bitcast.162), calls=%async_computation.16 | async-start | bytes 8388608
  134.4 15.7 %copy-start.32 = (f32[128,16,128]{2,1,0:T(8,128)S(1)}, f32[128,16,128]{2,1,0:T(8,128)}, u32[]{:S(2)}) copy-start(f32[128,16,128]{2,1,0:T(8,128)} %gather_fusion.29) | copy-start | bytes 3145732
  134.4 31.5 %slice-start.13 = ((s8[8388608]{0:T(1024)(128)(4,1)}), s8[4194304]{0:T(1024)(128)(4,1)S(1)}, s32[]{:S(2)}) async-start(s8[8388608]{0:T(1024)(128)(4,1)} %bitcast.162), calls=%async_computation.17 | async-start | bytes 8388608
  134.4 44.6 %slice-start.10 = ((s8[8388608]{0:T(1024)(128)(4,1)}), s8[4194304]{0:T(1024)(128)(4,1)S(1)}, s32[]{:S(2)}) async-start(s8[8388608]{0:T(1024)(128)(4,1)} %bitcast.160), calls=%async_computation.14 | async-start | bytes 8388608
  150.1 15.8 %copy-start.31 = (f32[128,16,128]{2,1,0:T(8,128)S(1)}, f32[128,16,128]{2,1,0:T(8,128)}, u32[]{:S(2)}) copy-start(f32[128,16,128]{2,1,0:T(8,128)} %gather_fusion.31) | copy-start | bytes 3145732
  150.2 28.9 %slice-start.11 = ((s8[8388608]{0:T(1024)(128)(4,1)}), s8[4194304]{0:T(1024)(128)(4,1)S(1)}, s32[]{:S(2)}) async-start(s8[8388608]{0:T(1024)(128)(4,1)} %bitcast.160), calls=%async_computation.15 | async-start | bytes 8388608
  150.2 43.4 %slice-start.8 = ((s8[8388608]{0:T(1024)(128)(4,1)}), s8[4194304]{0:T(1024)(128)(4,1)S(1)}, s32[]{:S(2)}) async-start(s8[8388608]{0:T(1024)(128)(4,1)} %bitcast.158), calls=%async_computation.12 | async-start | bytes 8388608
  165.9 13.1 %copy-start.30 = (f32[128,16,128]{2,1,0:T(8,128)S(1)}, f32[128,16,128]{2,1,0:T(8,128)}, u32[]{:S(2)}) copy-start(f32[128,16,128]{2,1,0:T(8,128)} %gather_fusion.33) | copy-start | bytes 3145732
  166.0 27.6 %slice-start.9 = ((s8[8388608]{0:T(1024)(128)(4,1)}), s8[4194304]{0:T(1024)(128)(4,1)S(1)}, s32[]{:S(2)}) async-start(s8[8388608]{0:T(1024)(128)(4,1)} %bitcast.158), calls=%async_computation.13 | async-start | bytes 8388608
  166.0 42.2 %slice-start.6 = ((s8[8388608]{0:T(1024)(128)(4,1)}), s8[4194304]{0:T(1024)(128)(4,1)S(1)}, s32[]{:S(2)}) async-start(s8[8388608]{0:T(1024)(128)(4,1)} %bitcast.156), calls=%async_computation.10 | async-start | bytes 8388608
  179.1 14.5 %copy-start.29 = (f32[128,16,128]{2,1,0:T(8,128)S(1)}, f32[128,16,128]{2,1,0:T(8,128)}, u32[]{:S(2)}) copy-start(f32[128,16,128]{2,1,0:T(8,128)} %gather_fusion.35) | copy-start | bytes 3145732
  179.1 29.1 %slice-start.7 = ((s8[8388608]{0:T(1024)(128)(4,1)}), s8[4194304]{0:T(1024)(128)(4,1)S(1)}, s32[]{:S(2)}) async-start(s8[8388608]{0:T(1024)(128)(4,1)} %bitcast.156), calls=%async_computation.11 | async-start | bytes 8388608
  179.1 42.2 %slice-start.4 = ((s8[8388608]{0:T(1024)(128)(4,1)}), s8[4194304]{0:T(1024)(128)(4,1)S(1)}, s32[]{:S(2)}) async-start(s8[8388608]{0:T(1024)(128)(4,1)} %bitcast.154), calls=%async_computation.8 | async-start | bytes 8388608
  193.5 14.6 %copy-start.28 = (f32[128,16,128]{2,1,0:T(8,128)S(1)}, f32[128,16,128]{2,1,0:T(8,128)}, u32[]{:S(2)}) copy-start(f32[128,16,128]{2,1,0:T(8,128)} %gather_fusion.37) | copy-start | bytes 3145732
  193.5 27.7 %slice-start.5 = ((s8[8388608]{0:T(1024)(128)(4,1)}), s8[4194304]{0:T(1024)(128)(4,1)S(1)}, s32[]{:S(2)}) async-start(s8[8388608]{0:T(1024)(128)(4,1)} %bitcast.154), calls=%async_computation.9 | async-start | bytes 8388608
  193.6 41.0 %slice-start.2 = ((s8[8388608]{0:T(1024)(128)(4,1)}), s8[4194304]{0:T(1024)(128)(4,1)S(1)}, s32[]{:S(2)}) async-start(s8[8388608]{0:T(1024)(128)(4,1)} %bitcast.152), calls=%async_computation.6 | async-start | bytes 8388608
  208.2 26.4 %slice-start.3 = ((s8[8388608]{0:T(1024)(128)(4,1)}), s8[4194304]{0:T(1024)(128)(4,1)S(1)}, s32[]{:S(2)}) async-start(s8[8388608]{0:T(1024)(128)(4,1)} %bitcast.152), calls=%async_computation.7 | async-start | bytes 8388608
  221.3 13.3 %copy-start.26 = (f32[128,16,128]{2,1,0:T(8,128)S(1)}, f32[128,16,128]{2,1,0:T(8,128)}, u32[]{:S(2)}) copy-start(f32[128,16,128]{2,1,0:T(8,128)} %gather_fusion.41) | copy-start | bytes 3145732
  221.3 26.8 %slice-start = ((s8[8388608]{0:T(1024)(128)(4,1)}), s8[4194304]{0:T(1024)(128)(4,1)S(1)}, s32[]{:S(2)}) async-start(s8[8388608]{0:T(1024)(128)(4,1)} %bitcast.150), calls=%async_computation.4 | async-start | bytes 8388608
  234.6 13.5 %slice-start.1 = ((s8[8388608]{0:T(1024)(128)(4,1)}), s8[4194304]{0:T(1024)(128)(4,1)S(1)}, s32[]{:S(2)}) async-start(s8[8388608]{0:T(1024)(128)(4,1)} %bitcast.150), calls=%async_computation.5 | async-start | bytes 8388608
  234.6 13.5 %copy-start.25 = (f32[128,16,128]{2,1,0:T(8,128)S(1)}, f32[128,16,128]{2,1,0:T(8,128)}, u32[]{:S(2)}) copy-start(f32[128,16,128]{2,1,0:T(8,128)} %gather_fusion.43) | copy-start | bytes 3145732
  293.9 13.3 %copy-start.24 = (f32[128,16,128]{2,1,0:T(8,128)S(1)}, f32[128,16,128]{2,1,0:T(8,128)}, u32[]{:S(2)}) copy-start(f32[128,16,128]{2,1,0:T(8,128)} %gather_fusion.45) | copy-start | bytes 3145732
  297.7 24.9 %copy-start.23 = (f32[128,16,128]{2,1,0:T(8,128)S(1)}, f32[128,16,128]{2,1,0:T(8,128)}, u32[]{:S(2)}) copy-start(f32[128,16,128]{2,1,0:T(8,128)} %gather_fusion.47) | copy-start | bytes 3145732
  299.9 42.5 %all-to-all-start.1 = ((f32[16,128,128]{2,1,0:T(8,128)}), f32[16,128,128]{2,1,0:T(8,128)S(1)}, u32[]{:S(2)}, u32[]{:S(2)}) async-start(f32[16,128,128]{2,1,0:T(8,128)} %convolution_add_fusion), calls=%async_computation.1 | async-start | bytes 2097152 | tf_op jit(solution)/shard_map/all_to_all | solution.py:34
  338.0 27.3 %copy-start.3 = (f32[128,2048]{1,0:T(8,128)S(1)}, f32[128,2048]{1,0:T(8,128)}, u32[]{:S(2)}) copy-start(f32[128,2048]{1,0:T(8,128)} %param.12) | copy-start | bytes 3145732
  338.0 27.3 %copy-start.35 = (s32[20,2048]{1,0:T(8,128)S(1)}, s32[20,2048]{1,0:T(8,128)}, u32[]{:S(2)}) copy-start(s32[20,2048]{1,0:T(8,128)} %param.23) | copy-start | bytes 491524
  338.0 27.3 %copy-start.36 = (s32[20,128]{1,0:T(8,128)S(1)}, s32[20,128]{1,0:T(8,128)}, u32[]{:S(2)}) copy-start(s32[20,128]{1,0:T(8,128)} %param.22) | copy-start | bytes 30724
  343.3 20.6 %all-to-all-start.3 = ((f32[16,8,2048]{2,0,1:T(8,128)}), f32[16,8,2048]{2,0,1:T(8,128)S(1)}, u32[]{:S(2)}, u32[]{:S(2)}) async-start(f32[16,8,2048]{2,0,1:T(8,128)} %copy.67), calls=%async_computation.3 | async-start | bytes 2097152 | tf_op jit(solution)/shard_map/all_to_all | solution.py:46
  349.8 153.1 %copy-start.1 = (f32[16,128,128]{2,1,0:T(8,128)S(1)}, f32[16,128,128]{2,1,0:T(8,128)}, u32[]{:S(2)}) copy-start(f32[16,128,128]{2,1,0:T(8,128)} %param.17) | copy-start | bytes 3145732
  (23 other events, 154.0 us)
where the time goes:
time: 511 us; the launch traced here: 503 us
  matrix products  196 us (38%)
  blocking collectives  129 us (25%)
  local copies, waits for them, and re-layouts  128 us (25%)
  starting transfers between devices  27.5 us (5%)
  other arithmetic  9.54 us (2%)
  waiting for transfers between devices  8.98 us (2%)
  between operations  5.43 us (1%)
    dot_general x12, matrix products, local(): jnp.einsum('ujq,jpq->ujp', lower[:, down_cols[:, h]], down_patterns[down_...  174 us
    psum x1, blocking collectives, local(): lax.psum((jnp.sum(vector * image), jnp.sum(vector * vector)), ('row', 'co...  65.9 us
    psum x1, blocking collectives, local(): energy = lax.psum(jnp.sum(residual * residual), ('row', 'col'))  62.7 us
    gather x12, local copies, waits for them, and re-layouts, local(): down_patterns[down_pats[:, h]]  51.9 us
    gather x12, local copies, waits for them, and re-layouts, local(): lower[:, down_cols[:, h]]  20.8 us
    dot_general x12, matrix products, local(): jnp.einsum('ipq,iqd->ipd', up_patterns[up_pats[:, h]], upper[up_cols[:, h...  19 us
    gather x12, local copies, waits for them, and re-layouts, local(): upper[up_cols[:, h]]  18.3 us
    gather x12, local copies, waits for them, and re-layouts, local(): up_patterns[up_pats[:, h]]  18.2 us
  transfers between devices with their start and end apart: 4, of which 1 were waited for; matrix products, arithmetic and copies ran while one was open for 57% of the time, Pallas kernels for 0%

commit v1 on v0

v1 whole, which is shorter than its diff:
```python
import jax
import jax.numpy as jnp
from jax import lax
from jax.experimental import pallas as pl
from jax.experimental.pallas import tpu as pltpu
from jax.sharding import PartitionSpec as P

MESH = pl.DeviceIdType.MESH
f32, bf16 = jnp.float32, jnp.bfloat16
BLK = 128
HOPS = 12
NPAT = 16
ZC = [(1, 0), (3, 1), (2, 0), (1, 1), (3, 0), (2, 1), (0, 1), (0, 0)]
YX = [(1, 1), (3, 1), (2, 1), (1, 0), (0, 1), (3, 0), (2, 0), (0, 0)]


def split(x):
    hi = x.astype(bf16)
    lo = (x - hi.astype(f32)).astype(bf16)
    return hi, lo


def total_of(x):
    return jnp.sum(x, axis=(0, 1), keepdims=True)


def kernel(
    v_hbm, prev_hbm, upat_hbm, dpat_hbm, upo_hbm, dno_hbm,
    beta_ref, hub_ref, ucols, upats, dcols, dpats,
    w_hbm, coef,
    v, prev, wbuf, upat, dpat, upo, dno,
    vl, vh, x1f, x1h, x1l, x2o, x2p, dw, phl, yd,
    uo, do, ul, dl, g1, g2, g3,
    lsem, xl_s, xl_r, xh_s, xh_r, z1_s, z1_r, y1_s, y1_r, z2_s, z2_r, y2_s, y2_r,
    u_s, u_r, d_s, d_r, g1_s, g1_r, g2_s, g2_r, g3_s, g3_r,
):
    r, c = lax.axis_index("row"), lax.axis_index("col")
    xhi, s = lax.div(r, 8), lax.rem(r, 8)
    z, core = lax.div(s, 2), lax.rem(s, 2)
    y, xlo = lax.div(c, 2), lax.rem(c, 2)
    rhi = (1 - xhi) * 8 + s
    clo = y * 2 + 1 - xlo
    dev_lo, dev_x3, dev_hi = (r, clo), (rhi, clo), (rhi, c)

    def zc_to(k):
        dz, dc = ZC[k]
        return lax.rem(z + dz, 4) * 2 + lax.rem(core + dc, 2)

    def zc_from(k):
        dz, dc = ZC[k]
        return lax.rem(z + 4 - dz, 4) * 2 + lax.rem(core + 2 - dc, 2)

    def yx_to(dy, dx):
        return lax.rem(y + dy, 4) * 2 + lax.rem(xlo + dx, 2)

    def yx_from(dy, dx):
        return lax.rem(y + 4 - dy, 4) * 2 + lax.rem(xlo + 2 - dx, 2)

    def cols_of(k):
        return pl.ds(pl.multiple_of(k * 256, 256), 256)

    def rows_of(k):
        return pl.ds(pl.multiple_of(k * 16, 16), 16)

    def remote(src, dst, ssem, rsem, dev):
        return pltpu.make_async_remote_copy(
            src_ref=src, dst_ref=dst, send_sem=ssem, recv_sem=rsem, device_id=dev, device_id_type=MESH
        )

    locals_ = [
        pltpu.make_async_copy(a, b, lsem.at[i])
        for i, (a, b) in enumerate(
            [
                (v_hbm, v),
                (upat_hbm, upat),
                (dpat_hbm, dpat),
                (upo_hbm, upo),
                (dno_hbm, dno),
                (prev_hbm, prev),
            ]
        )
    ]
    barrier = pltpu.get_barrier_semaphore()
    peers = [(xhi * 8 + zc_to(k), c) for k in range(7)]
    peers += [(r, yx_to(dy, dx)) for dy, dx in YX[:7]]
    peers += [dev_x3, dev_hi]
    for dev in peers:
        pl.semaphore_signal(barrier, inc=1, device_id=dev, device_id_type=MESH)
    for cp in locals_:
        cp.start()
    pl.semaphore_wait(barrier, len(peers))

    started = []

    def go(cp):
        cp.start()
        started.append(cp)
        return cp

    to = [zc_to(k) for k in range(8)]
    frm = [zc_from(k) for k in range(8)]

    def send_x(k):
        return go(remote(v_hbm.at[:, cols_of(to[k])], vl.at[to[k]], xl_s.at[k], xl_r.at[k], dev_lo))

    xl = [send_x(0), send_x(1)]
    z1, y1 = [], []
    for k in range(7):
        z1.append(
            go(remote(v_hbm.at[:, cols_of(to[k])], x1f.at[r], z1_s.at[k], z1_r.at[k], (xhi * 8 + to[k], c)))
        )
        if k < 3:
            dy = (1, 3, 2)[k]
            cp = yx_to(dy, 0)
            y1.append(go(remote(v_hbm.at[rows_of(cp)], x2o.at[y], y1_s.at[k], y1_r.at[k], (r, cp))))

    locals_[1].wait()
    locals_[2].wait()

    def prep(t, _):
        hi, lo = split(upat[t])
        phl[t, 0:BLK] = hi
        phl[t, BLK : 2 * BLK] = lo
        hi, lo = split(dpat[t].T)
        dw[t, 0:BLK] = hi
        dw[t, BLK : 2 * BLK] = hi
        dw[t, 2 * BLK : 3 * BLK] = lo
        return 0

    lax.fori_loop(0, NPAT, prep, 0)
    locals_[0].wait()

    def make_base():
        locals_[3].wait()
        locals_[4].wait()
        ups = upo[...].astype(f32).T
        hub = hub_ref[0]

        def step(i, acc):
            cs = pl.ds(pl.multiple_of(i * 256, 256), 256)
            both = jnp.dot(ups, dno[:, cs].astype(f32), preferred_element_type=f32)
            vv = v[:, cs]
            wbuf[:, cs] = hub * both * vv
            sq = vv * vv
            return acc + sum(sq[8 * a : 8 * a + 8] for a in range(16))

        acc = lax.fori_loop(0, 8, step, jnp.zeros((8, 256), f32))
        return total_of(acc)

    def products(xs, k0s, n):
        hi, lo = split(xs)
        lhs = jnp.concatenate([hi, lo, hi], axis=1)

        def step(i, _):
            rhs = jnp.concatenate([dw[i * 4 + a] for a in range(4)], axis=1)
            out = jnp.dot(lhs, rhs, preferred_element_type=f32)
            for a in range(4):
                for b, k0 in enumerate(k0s):
                    part = out[b * n * 16 : (b + 1) * n * 16, a * BLK : (a + 1) * BLK]
                    yd[i * 4 + a, pl.ds(k0, n)] = part.reshape(n, 16, BLK)
            return 0

        lax.fori_loop(0, NPAT // 4, step, 0)

    def own_products(ysrc, ref):
        xs = jnp.concatenate([ref[:, j * BLK : (j + 1) * BLK] for j in range(16)], axis=0)
        products(xs, [(ysrc * 2 + xlo) * 16], 16)

    def lo_products(k):
        for i in range(3):
            y2[k][i].wait_recv()
        xs, k0s = [], []
        for dy in range(4):
            ysrc = lax.rem(y + 4 - dy, 4)
            if dy == 0:
                piece = vl[to[k], rows_of(c)]
            else:
                piece = x2p[ysrc, to[k]]
            xs += [piece[:, 0:BLK], piece[:, BLK : 2 * BLK]]
            k0s.append((ysrc * 2 + 1 - xlo) * 16 + to[k] * 2)
        products(jnp.concatenate(xs, axis=0), k0s, 2)

    def convert(b, x):
        hi, lo = split(x)
        x1h[b] = hi
        x1l[b] = lo

    xh, z2, y2 = [], [], []

    def relay_hi(k):
        xh[k].wait_recv()
        if k < 7:
            z2.append(go(remote(vh.at[to[k]], x1f.at[rhi], z2_s.at[k], z2_r.at[k], (xhi * 8 + to[k], c))))

    sum_vv = None
    for k in range(8):
        xl[k].wait_recv()
        if k + 2 < 8:
            xl.append(send_x(k + 2))
        xh.append(go(remote(vl.at[to[k]], vh.at[to[k]], xh_s.at[k], xh_r.at[k], dev_x3)))
        row = []
        for i, dy in enumerate((1, 3, 2)):
            cp = yx_to(dy, 0)
            row.append(
                go(remote(vl.at[to[k], rows_of(cp)], x2p.at[y, to[k]], y2_s.at[k, i], y2_r.at[k, i], (r, cp)))
            )
        y2.append(row)
        if k >= 1:
            relay_hi(k - 1)
        if k == 0:
            sum_vv = make_base()
        if k == 1:
            own_products(y, v.at[rows_of(c)])
            convert(r, v[:, cols_of(s)])
        if 2 <= k <= 4:
            i = k - 2
            y1[i].wait_recv()
            ysrc = lax.rem(y + 4 - (1, 3, 2)[i], 4)
            own_products(ysrc, x2o.at[ysrc])
        if k >= 4:
            lo_products(k - 4)
        if k >= 5:
            for i in {5: (0, 1, 2), 6: (3, 4), 7: (5, 6)}[k]:
                z1[i].wait_recv()
                b = xhi * 8 + frm[i]
                convert(b, x1f[b])
    for k in range(4, 8):
        lo_products(k)

    sends_d = []
    for j, (dy, dx) in enumerate(YX):
        cp = yx_to(dy, dx)
        dst = do.at[j] if j < 7 else dl.at[c]

        def block(q, _, cp=cp, dst=dst):
            row = cp * 16 + q
            acc = yd[dpats[row, 0], dcols[row, 0]]
            for h in range(1, HOPS):
                acc = acc + yd[dpats[row, h], dcols[row, h]]
            dst[q] = acc
            return 0

        lax.fori_loop(0, 16, block, 0)
        if j < 7:
            sends_d.append(go(remote(do.at[j], dl.at[c], d_s.at[j], d_r.at[j], (r, cp))))

    for k in range(7):
        z2[k].wait_recv()
        b = (1 - xhi) * 8 + frm[k]
        convert(b, x1f[b])
    relay_hi(7)
    convert(rhi, vh[s])

    sends_u = []
    for j in range(8):
        row = xhi * 8 + to[j]
        lhs = jnp.concatenate([phl[upats[row, h]] for h in range(HOPS)], axis=1)
        rhs = jnp.concatenate([x1h[ucols[row, h]] for h in range(HOPS)], axis=0)
        a = jnp.dot(lhs, rhs, preferred_element_type=f32)
        rhs = jnp.concatenate([x1l[ucols[row, h]] for h in range(HOPS)], axis=0)
        b = jnp.dot(lhs[0:BLK], rhs, preferred_element_type=f32)
        out = a[0:BLK] + a[BLK : 2 * BLK] + b
        if j < 7:
            uo[j] = out
            sends_u.append(go(remote(uo.at[j], ul.at[s], u_s.at[j], u_r.at[j], (xhi * 8 + to[j], c))))
        else:
            ul[s] = out

    for cp in sends_d:
        cp.wait_recv()
    locals_[5].wait()
    for cp in sends_u:
        cp.wait_recv()

    beta = beta_ref[0]

    def image(i, accs):
        vi, vw = accs
        rs = pl.ds(pl.multiple_of(i * 16, 16), 16)
        for j in range(16):
            cs = slice(j * BLK, (j + 1) * BLK)
            hs = slice((j % 2) * BLK, (j % 2) * BLK + BLK)
            im = ul[j // 2, rs, hs] + dl[i, j] + wbuf[rs, cs]
            w = im - beta * prev[rs, cs]
            wbuf[rs, cs] = w
            vv = v[rs, cs]
            vi = vi + vv * im
            vw = vw + vv * w
        return vi, vw

    zero = jnp.zeros((16, BLK), f32)
    vi, vw = lax.fori_loop(0, 8, image, (zero, zero))
    out_cp = pltpu.make_async_copy(wbuf, w_hbm, lsem.at[6])
    out_cp.start()
    sum_vi, sum_vw = total_of(vi), total_of(vw)
    a_loc = jnp.where(sum_vv > 0.0, sum_vw / jnp.where(sum_vv > 0.0, sum_vv, 1.0), 0.0)

    def rest(i, accs):
        rr, rv = accs
        rs = pl.ds(pl.multiple_of(i * 16, 16), 16)
        for j in range(16):
            cs = slice(j * BLK, (j + 1) * BLK)
            vv = v[rs, cs]
            res = wbuf[rs, cs] - a_loc * vv
            rr = rr + res * res
            rv = rv + res * vv
        return rr, rv

    rr, rv = lax.fori_loop(0, 8, rest, (zero, zero))
    stats = [sum_vi, sum_vv, total_of(rr), total_of(rv), a_loc]
    stats = [jnp.broadcast_to(x, (1, BLK)) for x in stats]

    def put(ref, idx, vals):
        for i, x in enumerate(vals):
            ref[idx, i : i + 1] = x

    def merge(ref, n):
        vis = sum(ref[i, 0:1] for i in range(n))
        vvs = sum(ref[i, 1:2] for i in range(n))
        vws = sum(ref[i, 4:5] * ref[i, 1:2] + ref[i, 3:4] for i in range(n))
        a = jnp.where(vvs > 0.0, vws / jnp.where(vvs > 0.0, vvs, 1.0), 0.0)
        rrs, rvs = 0.0, 0.0
        for i in range(n):
            d = a - ref[i, 4:5]
            rrs = rrs + (ref[i, 2:3] - 2.0 * d * ref[i, 3:4] + d * d * ref[i, 1:2])
            rvs = rvs + (ref[i, 3:4] - d * ref[i, 1:2])
        return [vis, vvs, rrs, rvs, a]

    def stage(ref, idx, devs, ss, rs):
        put(ref, idx, stats)
        cps = [go(remote(ref.at[idx], ref.at[idx], ss.at[i], rs.at[i], d)) for i, d in enumerate(devs)]
        for cp in cps:
            cp.wait_recv()
        return merge(ref, len(devs) + 1)

    stats = stage(g1, s, [(xhi * 8 + to[k], c) for k in range(7)], g1_s, g1_r)
    stats = stage(g2, c, [(r, yx_to(dy, dx)) for dy, dx in YX[:7]], g2_s, g2_r)
    stats = stage(g3, xhi, [dev_hi], g3_s, g3_r)
    vis, vvs, rrs, rvs, a = stats
    alpha = vis / vvs
    d = alpha - a
    energy = rrs - 2.0 * d * rvs + d * d * vvs
    scale = jnp.sqrt(energy / (2048 * 16384) + 1e-06)
    coef[...] = jnp.concatenate([alpha, scale, jnp.zeros((6, BLK), f32)], axis=0)
    for cp in started:
        cp.wait_send()
    out_cp.wait()


def local(
    vector, previous, beta_prev, hubbard_u, up_patterns, down_patterns,
    up_cols, up_pats, down_cols, down_pats, up_occupied, down_occupied,
):
    hbm = pl.BlockSpec(memory_space=pl.ANY)
    smem = pl.BlockSpec(memory_space=pltpu.SMEM)
    vmem = pl.BlockSpec(memory_space=pltpu.VMEM)
    dma = pltpu.SemaphoreType.DMA
    vm = pltpu.VMEM
    w, coef = pl.pallas_call(
        kernel,
        name="lanczos_step",
        out_shape=(
            jax.ShapeDtypeStruct((128, 2048), f32),
            jax.ShapeDtypeStruct((8, BLK), f32),
        ),
        in_specs=[hbm] * 6 + [smem] * 6,
        out_specs=(hbm, vmem),
        scratch_shapes=[
            vm((128, 2048), f32),
            vm((128, 2048), f32),
            vm((128, 2048), f32),
            vm((NPAT, BLK, BLK), f32),
            vm((NPAT, BLK, BLK), f32),
            vm((20, BLK), jnp.int32),
            vm((20, 2048), jnp.int32),
            vm((8, BLK, 256), f32),
            vm((8, BLK, 256), f32),
            vm((16, BLK, 256), f32),
            vm((16, BLK, 256), bf16),
            vm((16, BLK, 256), bf16),
            vm((4, 16, 2048), f32),
            vm((4, 8, 16, 256), f32),
            vm((NPAT, 3 * BLK, BLK), bf16),
            vm((NPAT, 2 * BLK, BLK), bf16),
            vm((NPAT, 128, 16, BLK), f32),
            vm((7, BLK, 256), f32),
            vm((7, 16, 16, BLK), f32),
            vm((8, BLK, 256), f32),
            vm((8, 16, 16, BLK), f32),
            vm((8, 8, BLK), f32),
            vm((8, 8, BLK), f32),
            vm((2, 8, BLK), f32),
            dma((7,)),
            dma((8,)), dma((8,)), dma((8,)), dma((8,)),
            dma((7,)), dma((7,)), dma((3,)), dma((3,)),
            dma((7,)), dma((7,)), dma((8, 3)), dma((8, 3)),
            dma((7,)), dma((7,)), dma((7,)), dma((7,)),
            dma((7,)), dma((7,)), dma((7,)), dma((7,)), dma((1,)), dma((1,)),
        ],
        compiler_params=pltpu.CompilerParams(
            collective_id=0, has_side_effects=True, vmem_limit_bytes=48 << 20
        ),
    )(
        vector, previous, up_patterns, down_patterns, up_occupied, down_occupied,
        beta_prev, hubbard_u, up_cols, up_pats, down_cols, down_pats,
    )
    alpha, scale = coef[0, 0], coef[1, 0]
    return ((w - alpha * vector) / scale, coef[0:2, 0])


def solution(mesh):
    in_specs = (
        P("row", "col"),
        P("row", "col"),
        P(),
        P(),
        P(),
        P(),
        P(),
        P(),
        P(),
        P(),
        P(None, "row"),
        P(None, "col"),
    )
    out_specs = (P("row", "col"), P())
    return jax.shard_map(local, mesh=mesh, in_specs=in_specs, out_specs=out_specs, check_vma=False)
```

time: 511 us -> 86.2 us (0.17); the launches traced: 503 us -> 84.9 us
  matrix products: 196 us -> 0 us
  blocking collectives: 129 us -> 0 us
  local copies, waits for them, and re-layouts: 128 us -> 8.55 us
  Pallas kernels: 0 us -> 72 us
  starting transfers between devices: 27.5 us -> 0 us
  waiting for transfers between devices: 8.98 us -> 0 us
  other arithmetic: 9.54 us -> 2.43 us
    dot_general x25 -> x0, matrix products: 196 us -> none  [the longest x12 174 us: local(): jnp.einsum('ujq,jpq->ujp', lower[:, down_cols[:, h]], down_patterns[down_...]
    psum x2 -> x0, blocking collectives: 129 us -> none  [the longest x1 65.9 us: local(): lax.psum((jnp.sum(vector * image), jnp.sum(vector * vector)), ('row', 'co...]
    gather x48 -> x0, local copies, waits for them, and re-layouts: 109 us -> none  [the longest x12 51.9 us: local(): down_patterns[down_pats[:, h]]]
    pallas_call x0 -> x1, Pallas kernels: none -> 72 us  [local(): pl.pallas_call(kernel, name='lanczos_step', out_shape=(jax.ShapeDtypeStru...]
    all_to_all x4 -> x0, starting transfers between devices: 27.5 us -> none  [the longest x1 9.07 us: local(): lax.all_to_all(vector, 'row', split_axis=1, concat_axis=0, tiled=True)]
    all_to_all x6 -> x0, local copies, waits for them, and re-layouts: 12.3 us -> none  [the longest x2 5.18 us: local(): lax.all_to_all(up_acc.reshape(up_blocks * block, width), 'row', split_axi...]
    all_to_all x4 -> x0, waiting for transfers between devices: 8.98 us -> none  [the longest x1 8.97 us: local(): lax.all_to_all(down_acc.reshape(thin_rows, down_blocks * block), 'col', s...]
  transfers between devices with their start and end apart: 4 -> 0, of which waited for: 1 -> 0; matrix products, arithmetic and copies ran while one was open for 57% -> 0% of each run, Pallas kernels for 0% -> 0%
where the time goes in v1:
time: 86.2 us; the launch traced here: 84.9 us
  Pallas kernels  72 us (84%)
  local copies, waits for them, and re-layouts  8.55 us (10%)
  other arithmetic  2.43 us (3%)
  between operations  1.97 us (2%)
    pallas_call x1, Pallas kernels, local(): pl.pallas_call(kernel, name='lanczos_step', out_shape=(jax.ShapeDtypeStru...  72 us
    unnamed x20, local copies, waits for them, and re-layouts  7.34 us
    div x1, other arithmetic, local(): return ((w - alpha * vector) / scale, coef[0:2, 0])  2.43 us

profile of v1, /device:TPU:1, one launch (start us, length us, event | category | flops | bytes accessed | tf_op | source)
XLA Modules:
  0.0 84.9 jit_solution(6695311903305363786)
XLA Ops:
  1.9 0.0 copy-start.8
  1.9 0.8 copy.16.dcols
  2.7 0.0 copy-done.8
  2.7 0.0 copy-start.5
  2.8 0.0 copy-start.6
  2.8 0.0 copy-start.7
  2.8 0.1 copy.17.dpats
  2.9 0.6 copy-done.5
  3.5 0.0 copy-done.6
  3.5 0.0 copy-done.7
  3.5 0.0 copy-start
  3.5 1.2 %copy-done = f32[128,2048]{1,0:T(8,128)S(1)} copy-done((f32[128,2048]{1,0:T(8,128)S(1)}, f32[128,2048]{1,0:T(8,128)}, u32[]{:S(2)}) %copy-start) | copy-done | bytes 1048600
  4.7 0.0 copy-start.1
  4.7 1.2 %copy-done.1 = f32[128,2048]{1,0:T(8,128)S(1)} copy-done((f32[128,2048]{1,0:T(8,128)S(1)}, f32[128,2048]{1,0:T(8,128)}, u32[]{:S(2)}) %copy-start.1) | copy-done | bytes 1048600
  5.9 0.0 copy-start.2
  5.9 1.2 %copy-done.2 = f32[16,128,128]{2,1,0:T(8,128)S(1)} copy-done((f32[16,128,128]{2,1,0:T(8,128)S(1)}, f32[16,128,128]{2,1,0:T(8,128)}, u32[]{:S(2)}) %copy-start.2) | copy-done | bytes 1048600
  7.2 0.0 copy-start.3
  7.2 1.2 %copy-done.3 = f32[16,128,128]{2,1,0:T(8,128)S(1)} copy-done((f32[16,128,128]{2,1,0:T(8,128)S(1)}, f32[16,128,128]{2,1,0:T(8,128)}, u32[]{:S(2)}) %copy-start.3) | copy-done | bytes 1048600
  8.4 0.0 copy-start.4
  8.4 0.9 %copy-done.4 = s32[20,2048]{1,0:T(8,128)S(1)} copy-done((s32[20,2048]{1,0:T(8,128)S(1)}, s32[20,2048]{1,0:T(8,128)}, u32[]{:S(2)}) %copy-start.4) | copy-done | bytes 163864
  9.3 72.0 %lanczos_step.1 = (f32[128,2048]{1,0:T(8,128)S(1)}, f32[8,128]{1,0:T(8,128)S(1)}) custom-call(f32[128,2048]{1,0:T(8,128)S(1)} %copy-done, f32[128,2048]{1,0:T(8,128)S(1)} %copy-done.1, f32[16,128,128]{2,1,0:T(8,128)S(1)} %copy-done.2, f32[16,128,128]{2,1,0:T(8,128)S(1)} %copy-done.3, s32[20,128]{1,0:T(8,128)S(1)} %copy-done.5, s32[20,2048]{1,0:T(8,128)S(1)} %copy-done.4, ...), custom_call_target="tpu_custom_call" | custom-call | tf_op jit(solution)/shard_map/lanczos_step/pallas_call | solution.py:359
  81.3 0.6 slice_reduce_fusion
  81.9 0.6 fusion
  82.5 2.4 %subtract_divide_fusion = f32[128,2048]{1,0:T(8,128)} fusion(f32[128,2048]{1,0:T(8,128)S(1)} %get-tuple-element.4, f32[128,2048]{1,0:T(8,128)S(1)} %copy-done, f32[]{:T(128)} %bitcast.1, f32[]{:T(128)} %bitcast), kind=kLoop, calls=%fused_computation | loop fusion | flops 786432 | bytes 3145736 | tf_op jit(solution)/shard_map/div | solution.py:408
Async XLA Ops:
  1.9 0.8 copy-start.8
  2.7 0.7 copy-start.5
  2.8 0.7 copy-start.6
  2.8 0.7 copy-start.7
  3.5 1.2 %copy-start = (f32[128,2048]{1,0:T(8,128)S(1)}, f32[128,2048]{1,0:T(8,128)}, u32[]{:S(2)}) copy-start(f32[128,2048]{1,0:T(8,128)} %v_hbm.1) | copy-start | bytes 3145732
  4.7 1.2 %copy-start.1 = (f32[128,2048]{1,0:T(8,128)S(1)}, f32[128,2048]{1,0:T(8,128)}, u32[]{:S(2)}) copy-start(f32[128,2048]{1,0:T(8,128)} %prev_hbm.1) | copy-start | bytes 3145732
  5.9 1.2 %copy-start.2 = (f32[16,128,128]{2,1,0:T(8,128)S(1)}, f32[16,128,128]{2,1,0:T(8,128)}, u32[]{:S(2)}) copy-start(f32[16,128,128]{2,1,0:T(8,128)} %upat_hbm.1) | copy-start | bytes 3145732
  7.2 1.2 %copy-start.3 = (f32[16,128,128]{2,1,0:T(8,128)S(1)}, f32[16,128,128]{2,1,0:T(8,128)}, u32[]{:S(2)}) copy-start(f32[16,128,128]{2,1,0:T(8,128)} %dpat_hbm.1) | copy-start | bytes 3145732
  8.4 0.9 %copy-start.4 = (s32[20,2048]{1,0:T(8,128)S(1)}, s32[20,2048]{1,0:T(8,128)}, u32[]{:S(2)}) copy-start(s32[20,2048]{1,0:T(8,128)} %dno_hbm.1) | copy-start | bytes 491524

commit v2 on v1

--- a/solution.py
+++ b/solution.py
@@ -8,8 +8,11 @@
 MESH = pl.DeviceIdType.MESH
 f32, bf16 = jnp.float32, jnp.bfloat16
 BLK = 128
+CID = 0
 HOPS = 12
 NPAT = 16
+AHEAD = 4
+EARLY = 3
 ZC = [(1, 0), (3, 1), (2, 0), (1, 1), (3, 0), (2, 1), (0, 1), (0, 0)]
 YX = [(1, 1), (3, 1), (2, 1), (1, 0), (0, 1), (3, 0), (2, 0), (0, 0)]
 
@@ -24,15 +27,19 @@
     return jnp.sum(x, axis=(0, 1), keepdims=True)
 
 
+def ratio(p, q):
+    return jnp.where(q > 0.0, p / jnp.where(q > 0.0, q, 1.0), 0.0)
+
+
 def kernel(
     v_hbm, prev_hbm, upat_hbm, dpat_hbm, upo_hbm, dno_hbm,
-    beta_ref, hub_ref, ucols, upats, dcols, dpats,
-    w_hbm, coef,
+    beta_ref, hub_ref, ucols, upats, didx,
+    out_hbm, coef,
     v, prev, wbuf, upat, dpat, upo, dno,
     vl, vh, x1f, x1h, x1l, x2o, x2p, dw, phl, yd,
-    uo, do, ul, dl, g1, g2, g3,
-    lsem, xl_s, xl_r, xh_s, xh_r, z1_s, z1_r, y1_s, y1_r, z2_s, z2_r, y2_s, y2_r,
-    u_s, u_r, d_s, d_r, g1_s, g1_r, g2_s, g2_r, g3_s, g3_r,
+    uo, do, ul, dl, g1, g2, g2s,
+    lsem, osem, xl_s, xl_r, xh_s, xh_r, z1_s, z1_r, y1_s, y1_r, z2_s, z2_r, y2_s, y2_r,
+    u_s, u_r, d_s, d_r, g1_s, g1_r, g2_s, g2_r,
 ):
     r, c = lax.axis_index("row"), lax.axis_index("col")
     xhi, s = lax.div(r, 8), lax.rem(r, 8)
@@ -40,7 +47,7 @@
     y, xlo = lax.div(c, 2), lax.rem(c, 2)
     rhi = (1 - xhi) * 8 + s
     clo = y * 2 + 1 - xlo
-    dev_lo, dev_x3, dev_hi = (r, clo), (rhi, clo), (rhi, c)
+    dev_lo, dev_x3 = (r, clo), (rhi, clo)
 
     def zc_to(k):
         dz, dc = ZC[k]
@@ -83,7 +90,7 @@
     barrier = pltpu.get_barrier_semaphore()
     peers = [(xhi * 8 + zc_to(k), c) for k in range(7)]
     peers += [(r, yx_to(dy, dx)) for dy, dx in YX[:7]]
-    peers += [dev_x3, dev_hi]
+    peers += [dev_x3]
     for dev in peers:
         pl.semaphore_signal(barrier, inc=1, device_id=dev, device_id_type=MESH)
     for cp in locals_:
@@ -92,6 +99,7 @@
 
     started = []
 
+
     def go(cp):
         cp.start()
         started.append(cp)
@@ -100,10 +108,14 @@
     to = [zc_to(k) for k in range(8)]
     frm = [zc_from(k) for k in range(8)]
 
-    def send_x(k):
-        return go(remote(v_hbm.at[:, cols_of(to[k])], vl.at[to[k]], xl_s.at[k], xl_r.at[k], dev_lo))
-
-    xl = [send_x(0), send_x(1)]
+    chunks = [(k, 0, BLK) for k in range(6)] + [(k, h, 64) for k in (6, 7) for h in (0, 64)]
+
+    def send_x(i):
+        k, h, n = chunks[i]
+        rs = pl.ds(h, n)
+        return go(remote(v_hbm.at[rs, cols_of(to[k])], vl.at[to[k], rs], xl_s.at[i], xl_r.at[i], dev_lo))
+
+    xl = [send_x(i) for i in range(AHEAD)]
     z1, y1 = [], []
     for k in range(7):
         z1.append(
@@ -157,7 +169,7 @@
             for a in range(4):
                 for b, k0 in enumerate(k0s):
                     part = out[b * n * 16 : (b + 1) * n * 16, a * BLK : (a + 1) * BLK]
-                    yd[i * 4 + a, pl.ds(k0, n)] = part.reshape(n, 16, BLK)
+                    yd[pl.ds((i * 4 + a) * 128 + k0, n)] = part.reshape(n, 16, BLK)
             return 0
 
         lax.fori_loop(0, NPAT // 4, step, 0)
@@ -187,72 +199,54 @@
 
     xh, z2, y2 = [], [], []
 
-    def relay_hi(k):
-        xh[k].wait_recv()
+    def relay_hi(i):
+        k, h, n = chunks[i]
+        xh[i].wait_recv()
+        if h + n == BLK and k < 7:
+            z2.append(go(remote(vh.at[to[k]], x1f.at[rhi], z2_s.at[k], z2_r.at[k], (xhi * 8 + to[k], c))))
+
+    def hi_convert(k):
         if k < 7:
-            z2.append(go(remote(vh.at[to[k]], x1f.at[rhi], z2_s.at[k], z2_r.at[k], (xhi * 8 + to[k], c))))
-
-    sum_vv = None
-    for k in range(8):
-        xl[k].wait_recv()
-        if k + 2 < 8:
-            xl.append(send_x(k + 2))
-        xh.append(go(remote(vl.at[to[k]], vh.at[to[k]], xh_s.at[k], xh_r.at[k], dev_x3)))
-        row = []
-        for i, dy in enumerate((1, 3, 2)):
-            cp = yx_to(dy, 0)
-            row.append(
-                go(remote(vl.at[to[k], rows_of(cp)], x2p.at[y, to[k]], y2_s.at[k, i], y2_r.at[k, i], (r, cp)))
-            )
-        y2.append(row)
-        if k >= 1:
-            relay_hi(k - 1)
-        if k == 0:
-            sum_vv = make_base()
-        if k == 1:
-            own_products(y, v.at[rows_of(c)])
-            convert(r, v[:, cols_of(s)])
-        if 2 <= k <= 4:
-            i = k - 2
-            y1[i].wait_recv()
-            ysrc = lax.rem(y + 4 - (1, 3, 2)[i], 4)
-            own_products(ysrc, x2o.at[ysrc])
-        if k >= 4:
-            lo_products(k - 4)
-        if k >= 5:
-            for i in {5: (0, 1, 2), 6: (3, 4), 7: (5, 6)}[k]:
-                z1[i].wait_recv()
-                b = xhi * 8 + frm[i]
-                convert(b, x1f[b])
-    for k in range(4, 8):
-        lo_products(k)
-
-    sends_d = []
-    for j, (dy, dx) in enumerate(YX):
-        cp = yx_to(dy, dx)
-        dst = do.at[j] if j < 7 else dl.at[c]
-
-        def block(q, _, cp=cp, dst=dst):
-            row = cp * 16 + q
-            acc = yd[dpats[row, 0], dcols[row, 0]]
-            for h in range(1, HOPS):
-                acc = acc + yd[dpats[row, h], dcols[row, h]]
-            dst[q] = acc
+            z2[k].wait_recv()
+            b = (1 - xhi) * 8 + frm[k]
+            convert(b, x1f[b])
+        else:
+            convert(rhi, vh[s])
+
+    def own_convert(i):
+        z1[i].wait_recv()
+        b = xhi * 8 + frm[i]
+        convert(b, x1f[b])
+
+    def y_job(i):
+        y1[i].wait_recv()
+        ysrc = lax.rem(y + 4 - (1, 3, 2)[i], 4)
+        own_products(ysrc, x2o.at[ysrc])
+
+    sends_d, sends_u = [], []
+
+    def down_share(j):
+        cp = yx_to(*YX[j])
+
+        def block(q, _):
+            for n in range(2):
+                row = cp * 16 + q * 2 + n
+                parts = []
+                for i in range(HOPS):
+                    parts.append(yd[didx[i, row]])
+                while len(parts) > 1:
+                    parts = [sum(parts[i : i + 2]) for i in range(0, len(parts), 2)]
+                if j < 7:
+                    do[j, q * 2 + n] = parts[0]
+                else:
+                    dl[c, q * 2 + n] = parts[0]
             return 0
 
-        lax.fori_loop(0, 16, block, 0)
+        lax.fori_loop(0, 8, block, 0)
         if j < 7:
             sends_d.append(go(remote(do.at[j], dl.at[c], d_s.at[j], d_r.at[j], (r, cp))))
 
-    for k in range(7):
-        z2[k].wait_recv()
-        b = (1 - xhi) * 8 + frm[k]
-        convert(b, x1f[b])
-    relay_hi(7)
-    convert(rhi, vh[s])
-
-    sends_u = []
-    for j in range(8):
+    def up_block(j):
         row = xhi * 8 + to[j]
         lhs = jnp.concatenate([phl[upats[row, h]] for h in range(HOPS)], axis=1)
         rhs = jnp.concatenate([x1h[ucols[row, h]] for h in range(HOPS)], axis=0)
@@ -265,6 +259,51 @@
             sends_u.append(go(remote(uo.at[j], ul.at[s], u_s.at[j], u_r.at[j], (xhi * 8 + to[j], c))))
         else:
             ul[s] = out
+
+    jobs = {
+        1: [lambda: y_job(0), lambda: y_job(1)],
+        2: [lambda: y_job(2), lambda: lo_products(0)],
+        3: [lambda: lo_products(1)] + [lambda i=i: own_convert(i) for i in range(3)],
+        4: [lambda: lo_products(2)] + [lambda i=i: own_convert(i) for i in range(3, 7)],
+        5: [lambda: lo_products(3), lambda: hi_convert(0), lambda: hi_convert(1)],
+        6: [lambda: lo_products(4)],
+        7: [lambda: hi_convert(2), lambda: hi_convert(3)],
+        8: [lambda: lo_products(5)],
+        9: [lambda: hi_convert(4)],
+    }
+    sum_vv = None
+    for i, (k, h, n) in enumerate(chunks):
+        rs = pl.ds(h, n)
+        xl[i].wait_recv()
+        if i + AHEAD < len(chunks):
+            xl.append(send_x(i + AHEAD))
+        xh.append(go(remote(vl.at[to[k], rs], vh.at[to[k], rs], xh_s.at[i], xh_r.at[i], dev_x3)))
+        if h + n == BLK:
+            row = []
+            for m, dy in enumerate((1, 3, 2)):
+                cp = yx_to(dy, 0)
+                src = vl.at[to[k], rows_of(cp)]
+                row.append(go(remote(src, x2p.at[y, to[k]], y2_s.at[k, m], y2_r.at[k, m], (r, cp))))
+            y2.append(row)
+        if i >= 1:
+            relay_hi(i - 1)
+        if i == 0:
+            sum_vv = make_base()
+            own_products(y, v.at[rows_of(c)])
+            convert(r, v[:, cols_of(s)])
+        for job in jobs.get(i, []):
+            job()
+    lo_products(6)
+    lo_products(7)
+    for j in range(EARLY):
+        down_share(j)
+    relay_hi(len(chunks) - 1)
+    for k in range(5, 8):
+        hi_convert(k)
+    for j in range(8):
+        up_block(j)
+        if j + EARLY < 8:
+            down_share(j + EARLY)
 
     for cp in sends_d:
         cp.wait_recv()
@@ -290,10 +329,8 @@
 
     zero = jnp.zeros((16, BLK), f32)
     vi, vw = lax.fori_loop(0, 8, image, (zero, zero))
-    out_cp = pltpu.make_async_copy(wbuf, w_hbm, lsem.at[6])
-    out_cp.start()
     sum_vi, sum_vw = total_of(vi), total_of(vw)
-    a_loc = jnp.where(sum_vv > 0.0, sum_vw / jnp.where(sum_vv > 0.0, sum_vv, 1.0), 0.0)
+    a_loc = ratio(sum_vw, sum_vv)
 
     def rest(i, accs):
         rr, rv = accs
@@ -308,43 +345,70 @@
 
     rr, rv = lax.fori_loop(0, 8, rest, (zero, zero))
     stats = [sum_vi, sum_vv, total_of(rr), total_of(rv), a_loc]
-    stats = [jnp.broadcast_to(x, (1, BLK)) for x in stats]
-
-    def put(ref, idx, vals):
+    lane = lax.broadcasted_iota(jnp.int32, (1, BLK), 1)
+
+    def row_of(vals):
+        row = jnp.zeros((1, BLK), f32)
         for i, x in enumerate(vals):
-            ref[idx, i : i + 1] = x
-
-    def merge(ref, n):
-        vis = sum(ref[i, 0:1] for i in range(n))
-        vvs = sum(ref[i, 1:2] for i in range(n))
-        vws = sum(ref[i, 4:5] * ref[i, 1:2] + ref[i, 3:4] for i in range(n))
-        a = jnp.where(vvs > 0.0, vws / jnp.where(vvs > 0.0, vvs, 1.0), 0.0)
-        rrs, rvs = 0.0, 0.0
-        for i in range(n):
-            d = a - ref[i, 4:5]
-            rrs = rrs + (ref[i, 2:3] - 2.0 * d * ref[i, 3:4] + d * d * ref[i, 1:2])
-            rvs = rvs + (ref[i, 3:4] - d * ref[i, 1:2])
-        return [vis, vvs, rrs, rvs, a]
-
-    def stage(ref, idx, devs, ss, rs):
-        put(ref, idx, stats)
-        cps = [go(remote(ref.at[idx], ref.at[idx], ss.at[i], rs.at[i], d)) for i, d in enumerate(devs)]
-        for cp in cps:
-            cp.wait_recv()
-        return merge(ref, len(devs) + 1)
-
-    stats = stage(g1, s, [(xhi * 8 + to[k], c) for k in range(7)], g1_s, g1_r)
-    stats = stage(g2, c, [(r, yx_to(dy, dx)) for dy, dx in YX[:7]], g2_s, g2_r)
-    stats = stage(g3, xhi, [dev_hi], g3_s, g3_r)
-    vis, vvs, rrs, rvs, a = stats
+            row = jnp.where(lane == i, x, row)
+        return row
+
+    def merge(t):
+        vis, vvs, rrs, rvs, a_s = [t[:, i : i + 1] for i in range(5)]
+
+        def add(x):
+            return jnp.sum(x, axis=0, keepdims=True)
+
+        vv = add(vvs)
+        a = ratio(add(a_s * vvs + rvs), vv)
+        d = a - a_s
+        return [add(vis), vv, add(rrs - 2.0 * d * rvs + d * d * vvs), add(rvs - d * vvs), a]
+
+    g1[core] = row_of(stats)
+    cp = go(remote(g1.at[core], g1.at[core], g1_s, g1_r, (xhi * 8 + z * 2 + 1 - core, c)))
+    cp.wait_recv()
+    stats = merge(jnp.concatenate([g1[0], g1[1]], axis=0))
+    x = xhi * 2 + xlo
+    chip = x * 16 + y * 4 + z
+    g2[chip] = row_of(stats)
+
+    def to_chip(i):
+        xx = lax.rem(x + lax.div(i, 16), 4)
+        yy = lax.rem(y + lax.rem(lax.div(i, 4), 4), 4)
+        zz = lax.rem(z + lax.rem(i, 4), 4)
+        dev = (lax.div(xx, 2) * 8 + zz * 2 + core, yy * 2 + lax.rem(xx, 2))
+        return remote(g2.at[chip], g2.at[chip], g2_s.at[i], g2_r.at[i], dev)
+
+    def all_chips(act):
+        def body(i, _):
+            act(to_chip(i))
+            return 0
+
+        lax.fori_loop(1, 64, body, 0)
+
+    all_chips(lambda cp: cp.start())
+    all_chips(lambda cp: cp.wait_recv())
+    for i in range(64):
+        g2s[i : i + 1] = g2[i]
+    vis, vvs, rrs, rvs, a = merge(g2s[...])
     alpha = vis / vvs
     d = alpha - a
     energy = rrs - 2.0 * d * rvs + d * d * vvs
     scale = jnp.sqrt(energy / (2048 * 16384) + 1e-06)
-    coef[...] = jnp.concatenate([alpha, scale, jnp.zeros((6, BLK), f32)], axis=0)
+    outs = []
+    for i in range(4):
+        rs = pl.ds(i * 32, 32)
+        wbuf[rs] = (wbuf[rs] - alpha * v[rs]) / scale
+        cp = pltpu.make_async_copy(wbuf.at[rs], out_hbm.at[rs], osem.at[i])
+        cp.start()
+        outs.append(cp)
+    coef[0] = alpha[0, 0]
+    coef[1] = scale[0, 0]
+    all_chips(lambda cp: cp.wait_send())
     for cp in started:
         cp.wait_send()
-    out_cp.wait()
+    for cp in outs:
+        cp.wait()
 
 
 def local(
@@ -353,18 +417,17 @@
 ):
     hbm = pl.BlockSpec(memory_space=pl.ANY)
     smem = pl.BlockSpec(memory_space=pltpu.SMEM)
-    vmem = pl.BlockSpec(memory_space=pltpu.VMEM)
     dma = pltpu.SemaphoreType.DMA
     vm = pltpu.VMEM
-    w, coef = pl.pallas_call(
+    return pl.pallas_call(
         kernel,
         name="lanczos_step",
         out_shape=(
             jax.ShapeDtypeStruct((128, 2048), f32),
-            jax.ShapeDtypeStruct((8, BLK), f32),
+            jax.ShapeDtypeStruct((2,), f32),
         ),
-        in_specs=[hbm] * 6 + [smem] * 6,
-        out_specs=(hbm, vmem),
+        in_specs=[hbm] * 6 + [smem] * 5,
+        out_specs=(hbm, smem),
         scratch_shapes=[
             vm((128, 2048), f32),
             vm((128, 2048), f32),
@@ -382,30 +445,28 @@
             vm((4, 8, 16, 256), f32),
             vm((NPAT, 3 * BLK, BLK), bf16),
             vm((NPAT, 2 * BLK, BLK), bf16),
-            vm((NPAT, 128, 16, BLK), f32),
+            vm((NPAT * 128, 16, BLK), f32),
             vm((7, BLK, 256), f32),
             vm((7, 16, 16, BLK), f32),
             vm((8, BLK, 256), f32),
             vm((8, 16, 16, BLK), f32),
-            vm((8, 8, BLK), f32),
-            vm((8, 8, BLK), f32),
-            vm((2, 8, BLK), f32),
-            dma((7,)),
-            dma((8,)), dma((8,)), dma((8,)), dma((8,)),
+            vm((2, 1, BLK), f32),
+            vm((64, 1, BLK), f32),
+            vm((64, BLK), f32),
+            dma((6,)), dma((4,)),
+            dma((10,)), dma((10,)), dma((10,)), dma((10,)),
             dma((7,)), dma((7,)), dma((3,)), dma((3,)),
             dma((7,)), dma((7,)), dma((8, 3)), dma((8, 3)),
             dma((7,)), dma((7,)), dma((7,)), dma((7,)),
-            dma((7,)), dma((7,)), dma((7,)), dma((7,)), dma((1,)), dma((1,)),
+            dma, dma, dma((64,)), dma((64,)),
         ],
         compiler_params=pltpu.CompilerParams(
-            collective_id=0, has_side_effects=True, vmem_limit_bytes=48 << 20
+            collective_id=CID, has_side_effects=True, vmem_limit_bytes=60 << 20
         ),
     )(
         vector, previous, up_patterns, down_patterns, up_occupied, down_occupied,
-        beta_prev, hubbard_u, up_cols, up_pats, down_cols, down_pats,
+        beta_prev, hubbard_u, up_cols, up_pats, (down_pats * 128 + down_cols).T,
     )
-    alpha, scale = coef[0, 0], coef[1, 0]
-    return ((w - alpha * vector) / scale, coef[0:2, 0])
 
 
 def solution(mesh):

time: 86.2 us -> 78.9 us (0.915)
  local copies, waits for them, and re-layouts: 8.55 us -> 2.81 us
  other arithmetic: 2.43 us -> 1.32 us
    unnamed x20 -> x4, local copies, waits for them, and re-layouts: 7.34 us -> 2.81 us
    div x1 -> x0, other arithmetic: 2.43 us -> none  [local(): return ((w - alpha * vector) / scale, coef[0:2, 0])]
    transpose x0 -> x1, other arithmetic: none -> 1.32 us  [local(): return pl.pallas_call(kernel, name='lanczos_step', out_shape=(jax.ShapeDt...]
    slice x2 -> x0, local copies, waits for them, and re-layouts: 1.21 us -> none  [the longest x1 0.63 us: local(): return ((w - alpha * vector) / scale, coef[0:2, 0])]
where the time goes in v2:
time: 78.9 us; the launch traced here: 78.3 us
  Pallas kernels  72.2 us (92%)
  local copies, waits for them, and re-layouts  2.81 us (4%)
  between operations  1.94 us (2%)
  other arithmetic  1.32 us (2%)
    pallas_call x1, Pallas kernels, local(): pl.pallas_call(kernel, name='lanczos_step', out_shape=(jax.ShapeDtypeStru...  72.2 us
    unnamed x4, local copies, waits for them, and re-layouts  2.81 us

profile of v2, /device:TPU:1, one launch (start us, length us, event | category | flops | bytes accessed | tf_op | source)
XLA Modules:
  0.0 78.3 jit_solution(11313862059873253028)
XLA Ops:
  1.9 1.3 %add_bitcast_fusion.didx = s32[12,128]{1,0:T(8,128)} fusion(s32[128,12]{0,1:T(8,128)} %param.20, s32[128,12]{0,1:T(8,128)} %param.21), kind=kLoop, calls=%fused_computation | loop fusion | flops 3072 | bytes 18432 | tf_op jit(solution)/shard_map/transpose | solution.py:468
  3.2 72.2 %lanczos_step.1 = (f32[128,2048]{1,0:T(8,128)}, f32[2]{0:T(128)}) custom-call(f32[128,2048]{1,0:T(8,128)} %v_hbm.1, f32[128,2048]{1,0:T(8,128)} %prev_hbm.1, f32[16,128,128]{2,1,0:T(8,128)} %upat_hbm.1, f32[16,128,128]{2,1,0:T(8,128)} %dpat_hbm.1, s32[20,128]{1,0:T(8,128)} %upo_hbm.1, s32[20,2048]{1,0:T(8,128)} %dno_hbm.1, f32[1]{0:T(128)S(6)} %copy.16.beta_ref, ...), custom_call_target="tpu_custom_call" | custom-call | tf_op jit(solution)/shard_map/lanczos_step/pallas_call | solution.py:422
  75.5 0.0 copy-start
  75.5 2.3 %copy.18 = f32[128,2048]{1,0:T(8,128)} copy(f32[128,2048]{1,0:T(8,128)} %get-tuple-element.4) | data formatting | bytes 2097152
  77.8 0.0 copy-done
  77.8 0.5 copy.19
Async XLA Ops:
  75.5 2.3 %copy-start = (f32[2]{0:T(128)S(1)}, f32[2]{0:T(128)}, u32[]{:S(2)}) copy-start(f32[2]{0:T(128)} %get-tuple-element.5) | copy-start | bytes 28

commit v3 on v2

--- a/solution.py
+++ b/solution.py
@@ -11,7 +11,7 @@
 CID = 0
 HOPS = 12
 NPAT = 16
-AHEAD = 4
+AHEAD = 10
 EARLY = 3
 ZC = [(1, 0), (3, 1), (2, 0), (1, 1), (3, 0), (2, 1), (0, 1), (0, 0)]
 YX = [(1, 1), (3, 1), (2, 1), (1, 0), (0, 1), (3, 0), (2, 0), (0, 0)]
@@ -33,7 +33,7 @@
 
 def kernel(
     v_hbm, prev_hbm, upat_hbm, dpat_hbm, upo_hbm, dno_hbm,
-    beta_ref, hub_ref, ucols, upats, didx,
+    beta_ref, hub_ref, ucols, upats, dcols, dpats,
     out_hbm, coef,
     v, prev, wbuf, upat, dpat, upo, dno,
     vl, vh, x1f, x1h, x1l, x2o, x2p, dw, phl, yd,
@@ -178,18 +178,19 @@
         xs = jnp.concatenate([ref[:, j * BLK : (j + 1) * BLK] for j in range(16)], axis=0)
         products(xs, [(ysrc * 2 + xlo) * 16], 16)
 
-    def lo_products(k):
-        for i in range(3):
-            y2[k][i].wait_recv()
+    def lo_products(*ks):
         xs, k0s = [], []
-        for dy in range(4):
-            ysrc = lax.rem(y + 4 - dy, 4)
-            if dy == 0:
-                piece = vl[to[k], rows_of(c)]
-            else:
-                piece = x2p[ysrc, to[k]]
-            xs += [piece[:, 0:BLK], piece[:, BLK : 2 * BLK]]
-            k0s.append((ysrc * 2 + 1 - xlo) * 16 + to[k] * 2)
+        for k in ks:
+            for i in range(3):
+                y2[k][i].wait_recv()
+            for dy in range(4):
+                ysrc = lax.rem(y + 4 - dy, 4)
+                if dy == 0:
+                    piece = vl[to[k], rows_of(c)]
+                else:
+                    piece = x2p[ysrc, to[k]]
+                xs += [piece[:, 0:BLK], piece[:, BLK : 2 * BLK]]
+                k0s.append((ysrc * 2 + 1 - xlo) * 16 + to[k] * 2)
         products(jnp.concatenate(xs, axis=0), k0s, 2)
 
     def convert(b, x):
@@ -233,7 +234,7 @@
                 row = cp * 16 + q * 2 + n
                 parts = []
                 for i in range(HOPS):
-                    parts.append(yd[didx[i, row]])
+                    parts.append(yd[dpats[i, row] * 128 + dcols[i, row]])
                 while len(parts) > 1:
                     parts = [sum(parts[i : i + 2]) for i in range(0, len(parts), 2)]
                 if j < 7:
@@ -262,13 +263,11 @@
 
     jobs = {
         1: [lambda: y_job(0), lambda: y_job(1)],
-        2: [lambda: y_job(2), lambda: lo_products(0)],
-        3: [lambda: lo_products(1)] + [lambda i=i: own_convert(i) for i in range(3)],
-        4: [lambda: lo_products(2)] + [lambda i=i: own_convert(i) for i in range(3, 7)],
-        5: [lambda: lo_products(3), lambda: hi_convert(0), lambda: hi_convert(1)],
-        6: [lambda: lo_products(4)],
+        2: [lambda: y_job(2)],
+        3: [lambda: lo_products(0, 1)] + [lambda i=i: own_convert(i) for i in range(3)],
+        4: [lambda i=i: own_convert(i) for i in range(3, 7)],
+        5: [lambda: lo_products(2, 3), lambda: hi_convert(0), lambda: hi_convert(1)],
         7: [lambda: hi_convert(2), lambda: hi_convert(3)],
-        8: [lambda: lo_products(5)],
         9: [lambda: hi_convert(4)],
     }
     sum_vv = None
@@ -293,8 +292,8 @@
             convert(r, v[:, cols_of(s)])
         for job in jobs.get(i, []):
             job()
-    lo_products(6)
-    lo_products(7)
+    lo_products(4, 5)
+    lo_products(6, 7)
     for j in range(EARLY):
         down_share(j)
     relay_hi(len(chunks) - 1)
@@ -308,27 +307,30 @@
     for cp in sends_d:
         cp.wait_recv()
     locals_[5].wait()
-    for cp in sends_u:
-        cp.wait_recv()
-
     beta = beta_ref[0]
-
-    def image(i, accs):
-        vi, vw = accs
-        rs = pl.ds(pl.multiple_of(i * 16, 16), 16)
-        for j in range(16):
-            cs = slice(j * BLK, (j + 1) * BLK)
-            hs = slice((j % 2) * BLK, (j % 2) * BLK + BLK)
-            im = ul[j // 2, rs, hs] + dl[i, j] + wbuf[rs, cs]
-            w = im - beta * prev[rs, cs]
-            wbuf[rs, cs] = w
-            vv = v[rs, cs]
-            vi = vi + vv * im
-            vw = vw + vv * w
-        return vi, vw
-
     zero = jnp.zeros((16, BLK), f32)
-    vi, vw = lax.fori_loop(0, 8, image, (zero, zero))
+    vi, vw = zero, zero
+    for k in (7, 0, 1, 2, 3, 4, 5, 6):
+        if k < 7:
+            sends_u[k].wait_recv()
+        place = frm[k]
+
+        def image(i, accs, place=place):
+            vi, vw = accs
+            rs = rows_of(i)
+            for n in range(2):
+                cs = pl.ds(pl.multiple_of(place * 256 + n * BLK, BLK), BLK)
+                im = ul[place, rs, n * BLK : (n + 1) * BLK] + dl[i, place * 2 + n] + wbuf[rs, cs]
+                w = im - beta * prev[rs, cs]
+                wbuf[rs, cs] = w
+                vv = v[rs, cs]
+                vi = vi + vv * im
+                vw = vw + vv * w
+            return vi, vw
+
+        vi, vw = lax.fori_loop(0, 8, image, (vi, vw))
+    out_cp = pltpu.make_async_copy(wbuf, out_hbm, osem)
+    out_cp.start()
     sum_vi, sum_vw = total_of(vi), total_of(vw)
     a_loc = ratio(sum_vw, sum_vv)
 
@@ -372,19 +374,21 @@
     chip = x * 16 + y * 4 + z
     g2[chip] = row_of(stats)
 
-    def to_chip(i):
-        xx = lax.rem(x + lax.div(i, 16), 4)
-        yy = lax.rem(y + lax.rem(lax.div(i, 4), 4), 4)
-        zz = lax.rem(z + lax.rem(i, 4), 4)
-        dev = (lax.div(xx, 2) * 8 + zz * 2 + core, yy * 2 + lax.rem(xx, 2))
-        return remote(g2.at[chip], g2.at[chip], g2_s.at[i], g2_r.at[i], dev)
-
     def all_chips(act):
         def body(i, _):
-            act(to_chip(i))
+            xx = lax.rem(x + lax.div(i, 4), 4)
+            yy = lax.rem(y + lax.rem(i, 4), 4)
+            base, col = lax.div(xx, 2) * 8 + core, yy * 2 + lax.rem(xx, 2)
+            for n in range(4):
+                dev = (base + lax.rem(z + n, 4) * 2, col)
+                cp = remote(g2.at[chip], g2.at[chip], g2_s.at[i * 4 + n], g2_r.at[i * 4 + n], dev)
+                if n > 0:
+                    act(cp)
+                else:
+                    pl.when(i > 0)(lambda cp=cp: act(cp))
             return 0
 
-        lax.fori_loop(1, 64, body, 0)
+        lax.fori_loop(0, 16, body, 0)
 
     all_chips(lambda cp: cp.start())
     all_chips(lambda cp: cp.wait_recv())
@@ -395,18 +399,33 @@
     d = alpha - a
     energy = rrs - 2.0 * d * rvs + d * d * vvs
     scale = jnp.sqrt(energy / (2048 * 16384) + 1e-06)
-    outs = []
-    for i in range(4):
-        rs = pl.ds(i * 32, 32)
-        wbuf[rs] = (wbuf[rs] - alpha * v[rs]) / scale
-        cp = pltpu.make_async_copy(wbuf.at[rs], out_hbm.at[rs], osem.at[i])
-        cp.start()
-        outs.append(cp)
     coef[0] = alpha[0, 0]
     coef[1] = scale[0, 0]
     all_chips(lambda cp: cp.wait_send())
     for cp in started:
         cp.wait_send()
+    out_cp.wait()
+
+
+def finish(w_hbm, v_hbm, coef, out_hbm, coef_out, w, v, sem):
+    parts = [pl.ds(i * 32, 32) for i in range(4)]
+    ins = [
+        [pltpu.make_async_copy(a.at[rs], b.at[rs], sem.at[n, i]) for n, (a, b) in enumerate(((w_hbm, w), (v_hbm, v)))]
+        for i, rs in enumerate(parts)
+    ]
+    for pair in ins:
+        for cp in pair:
+            cp.start()
+    alpha, scale = coef[0], coef[1]
+    coef_out[0] = alpha
+    coef_out[1] = scale
+    outs = []
+    for i, rs in enumerate(parts):
+        for cp in ins[i]:
+            cp.wait()
+        w[rs] = (w[rs] - alpha * v[rs]) / scale
+        outs.append(pltpu.make_async_copy(w.at[rs], out_hbm.at[rs], sem.at[2, i]))
+        outs[i].start()
     for cp in outs:
         cp.wait()
 
@@ -419,14 +438,14 @@
     smem = pl.BlockSpec(memory_space=pltpu.SMEM)
     dma = pltpu.SemaphoreType.DMA
     vm = pltpu.VMEM
-    return pl.pallas_call(
+    w, coef = pl.pallas_call(
         kernel,
         name="lanczos_step",
         out_shape=(
             jax.ShapeDtypeStruct((128, 2048), f32),
             jax.ShapeDtypeStruct((2,), f32),
         ),
-        in_specs=[hbm] * 6 + [smem] * 5,
+        in_specs=[hbm] * 6 + [smem] * 6,
         out_specs=(hbm, smem),
         scratch_shapes=[
             vm((128, 2048), f32),
@@ -453,7 +472,7 @@
             vm((2, 1, BLK), f32),
             vm((64, 1, BLK), f32),
             vm((64, BLK), f32),
-            dma((6,)), dma((4,)),
+            dma((6,)), dma,
             dma((10,)), dma((10,)), dma((10,)), dma((10,)),
             dma((7,)), dma((7,)), dma((3,)), dma((3,)),
             dma((7,)), dma((7,)), dma((8, 3)), dma((8, 3)),
@@ -465,8 +484,20 @@
         ),
     )(
         vector, previous, up_patterns, down_patterns, up_occupied, down_occupied,
-        beta_prev, hubbard_u, up_cols, up_pats, (down_pats * 128 + down_cols).T,
+        beta_prev, hubbard_u, up_cols, up_pats, down_cols.T, down_pats.T,
     )
+    return pl.pallas_call(
+        finish,
+        name="scale_residual",
+        out_shape=(
+            jax.ShapeDtypeStruct((128, 2048), f32),
+            jax.ShapeDtypeStruct((2,), f32),
+        ),
+        in_specs=[hbm, hbm, smem],
+        out_specs=(hbm, smem),
+        scratch_shapes=[vm((128, 2048), f32), vm((128, 2048), f32), dma((3, 4))],
+        compiler_params=pltpu.CompilerParams(vmem_limit_bytes=60 << 20),
+    )(w, vector, coef)
 
 
 def solution(mesh):

time: 78.9 us -> 77.7 us (0.985)
  Pallas kernels: 72.2 us -> 75.3 us
  local copies, waits for them, and re-layouts: 2.81 us -> 0 us
  other arithmetic: 1.32 us -> 0 us
    pallas_call x0 -> x1, Pallas kernels: none -> 3.52 us  [local(): pl.pallas_call(finish, name='scale_residual', out_shape=(jax.ShapeDtypeSt...]
    unnamed x4 -> x0, local copies, waits for them, and re-layouts: 2.81 us -> none
    transpose x1 -> x0, other arithmetic: 1.32 us -> none  [local(): return pl.pallas_call(kernel, name='lanczos_step', out_shape=(jax.ShapeDt...]
where the time goes in v3:
time: 77.7 us; the launch traced here: 77.2 us
  Pallas kernels  75.3 us (97%)
  between operations  1.93 us (2%)
    pallas_call x1, Pallas kernels, local(): pl.pallas_call(kernel, name='lanczos_step', out_shape=(jax.ShapeDtypeStru...  71.8 us
    pallas_call x1, Pallas kernels, local(): pl.pallas_call(finish, name='scale_residual', out_shape=(jax.ShapeDtypeSt...  3.52 us

profile of v3, /device:TPU:1, one launch (start us, length us, event | category | flops | bytes accessed | tf_op | source)
XLA Modules:
  0.0 77.2 jit_solution(11754018098864683795)
XLA Ops:
  1.9 71.8 %lanczos_step.1 = (f32[128,2048]{1,0:T(8,128)}, f32[2]{0:T(128)}) custom-call(f32[128,2048]{1,0:T(8,128)} %v_hbm.3, f32[128,2048]{1,0:T(8,128)} %prev_hbm.1, f32[16,128,128]{2,1,0:T(8,128)} %upat_hbm.1, f32[16,128,128]{2,1,0:T(8,128)} %dpat_hbm.1, s32[20,128]{1,0:T(8,128)} %upo_hbm.1, s32[20,2048]{1,0:T(8,128)} %dno_hbm.1, f32[1]{0:T(128)S(6)} %copy.14.beta_ref, ...), custom_call_target="tpu_custom_call" | custom-call | tf_op jit(solution)/shard_map/lanczos_step/pallas_call | solution.py:441
  73.7 3.5 %scale_residual.1 = (f32[128,2048]{1,0:T(8,128)}, f32[2]{0:T(128)}) custom-call(f32[128,2048]{1,0:T(8,128)} %get-tuple-element.4.w_hbm, f32[128,2048]{1,0:T(8,128)} %v_hbm.3, f32[2]{0:T(128)} %get-tuple-element.5.coef), custom_call_target="tpu_custom_call" | custom-call | tf_op jit(solution)/shard_map/scale_residual/pallas_call | solution.py:489

commit v4 on v3

--- a/solution.py
+++ b/solution.py
@@ -93,7 +93,7 @@
     peers += [dev_x3]
     for dev in peers:
         pl.semaphore_signal(barrier, inc=1, device_id=dev, device_id_type=MESH)
-    for cp in locals_:
+    for cp in locals_[:5]:
         cp.start()
     pl.semaphore_wait(barrier, len(peers))
 
@@ -262,10 +262,10 @@
             ul[s] = out
 
     jobs = {
-        1: [lambda: y_job(0), lambda: y_job(1)],
-        2: [lambda: y_job(2)],
-        3: [lambda: lo_products(0, 1)] + [lambda i=i: own_convert(i) for i in range(3)],
-        4: [lambda i=i: own_convert(i) for i in range(3, 7)],
+        1: [lambda: y_job(0)],
+        2: [lambda: y_job(1)],
+        3: [lambda: y_job(2)] + [lambda i=i: own_convert(i) for i in range(3)],
+        4: [lambda: lo_products(0, 1)] + [lambda i=i: own_convert(i) for i in range(3, 7)],
         5: [lambda: lo_products(2, 3), lambda: hi_convert(0), lambda: hi_convert(1)],
         7: [lambda: hi_convert(2), lambda: hi_convert(3)],
         9: [lambda: hi_convert(4)],
@@ -287,6 +287,7 @@
         if i >= 1:
             relay_hi(i - 1)
         if i == 0:
+            locals_[5].start()
             sum_vv = make_base()
             own_products(y, v.at[rows_of(c)])
             convert(r, v[:, cols_of(s)])

time: 77.7 us -> 77.2 us (level)
  no operation moved by 1% of the time
where the time goes in v4:
time: 77.2 us; the launch traced here: 76.9 us
  Pallas kernels  75 us (97%)
  between operations  1.93 us (2%)
    pallas_call x1, Pallas kernels, local(): pl.pallas_call(kernel, name='lanczos_step', out_shape=(jax.ShapeDtypeStru...  71.5 us
    pallas_call x1, Pallas kernels, local(): pl.pallas_call(finish, name='scale_residual', out_shape=(jax.ShapeDtypeSt...  3.52 us

profile of v4, /device:TPU:1, one launch (start us, length us, event | category | flops | bytes accessed | tf_op | source)
XLA Modules:
  0.0 76.9 jit_solution(12481174380004946023)
XLA Ops:
  1.9 71.5 %lanczos_step.1 = (f32[128,2048]{1,0:T(8,128)}, f32[2]{0:T(128)}) custom-call(f32[128,2048]{1,0:T(8,128)} %v_hbm.3, f32[128,2048]{1,0:T(8,128)} %prev_hbm.1, f32[16,128,128]{2,1,0:T(8,128)} %upat_hbm.1, f32[16,128,128]{2,1,0:T(8,128)} %dpat_hbm.1, s32[20,128]{1,0:T(8,128)} %upo_hbm.1, s32[20,2048]{1,0:T(8,128)} %dno_hbm.1, f32[1]{0:T(128)S(6)} %copy.14.beta_ref, ...), custom_call_target="tpu_custom_call" | custom-call | tf_op jit(solution)/shard_map/lanczos_step/pallas_call | solution.py:442
  73.4 3.5 %scale_residual.1 = (f32[128,2048]{1,0:T(8,128)}, f32[2]{0:T(128)}) custom-call(f32[128,2048]{1,0:T(8,128)} %get-tuple-element.4.w_hbm, f32[128,2048]{1,0:T(8,128)} %v_hbm.3, f32[2]{0:T(128)} %get-tuple-element.5.coef), custom_call_target="tpu_custom_call" | custom-call | tf_op jit(solution)/shard_map/scale_residual/pallas_call | solution.py:490

commit v5 on v4

--- a/solution.py
+++ b/solution.py
@@ -230,20 +230,20 @@
         cp = yx_to(*YX[j])
 
         def block(q, _):
-            for n in range(2):
-                row = cp * 16 + q * 2 + n
+            for n in range(4):
+                row = cp * 16 + q * 4 + n
                 parts = []
                 for i in range(HOPS):
                     parts.append(yd[dpats[i, row] * 128 + dcols[i, row]])
                 while len(parts) > 1:
                     parts = [sum(parts[i : i + 2]) for i in range(0, len(parts), 2)]
                 if j < 7:
-                    do[j, q * 2 + n] = parts[0]
+                    do[j, q * 4 + n] = parts[0]
                 else:
-                    dl[c, q * 2 + n] = parts[0]
+                    dl[c, q * 4 + n] = parts[0]
             return 0
 
-        lax.fori_loop(0, 8, block, 0)
+        lax.fori_loop(0, 4, block, 0)
         if j < 7:
             sends_d.append(go(remote(do.at[j], dl.at[c], d_s.at[j], d_r.at[j], (r, cp))))
 

time: 77.2 us -> 76.8 us (level)
  no operation moved by 1% of the time
where the time goes in v5:
time: 76.8 us; the launch traced here: 76.6 us
  Pallas kernels  74.7 us (97%)
  between operations  1.93 us (3%)
    pallas_call x1, Pallas kernels, local(): pl.pallas_call(kernel, name='lanczos_step', out_shape=(jax.ShapeDtypeStru...  71.2 us
    pallas_call x1, Pallas kernels, local(): pl.pallas_call(finish, name='scale_residual', out_shape=(jax.ShapeDtypeSt...  3.52 us

profile of v5, /device:TPU:1, one launch (start us, length us, event | category | flops | bytes accessed | tf_op | source)
XLA Modules:
  0.0 76.6 jit_solution(11915128558970518674)
XLA Ops:
  1.9 71.2 %lanczos_step.1 = (f32[128,2048]{1,0:T(8,128)}, f32[2]{0:T(128)}) custom-call(f32[128,2048]{1,0:T(8,128)} %v_hbm.3, f32[128,2048]{1,0:T(8,128)} %prev_hbm.1, f32[16,128,128]{2,1,0:T(8,128)} %upat_hbm.1, f32[16,128,128]{2,1,0:T(8,128)} %dpat_hbm.1, s32[20,128]{1,0:T(8,128)} %upo_hbm.1, s32[20,2048]{1,0:T(8,128)} %dno_hbm.1, f32[1]{0:T(128)S(6)} %copy.14.beta_ref, ...), custom_call_target="tpu_custom_call" | custom-call | tf_op jit(solution)/shard_map/lanczos_step/pallas_call | solution.py:442
  73.1 3.5 %scale_residual.1 = (f32[128,2048]{1,0:T(8,128)}, f32[2]{0:T(128)}) custom-call(f32[128,2048]{1,0:T(8,128)} %get-tuple-element.4.w_hbm, f32[128,2048]{1,0:T(8,128)} %v_hbm.3, f32[2]{0:T(128)} %get-tuple-element.5.coef), custom_call_target="tpu_custom_call" | custom-call | tf_op jit(solution)/shard_map/scale_residual/pallas_call | solution.py:490
